TPU v7x, 256 devices: a whole 4x4x8 slice. The times are simulated.
256 devices in a mesh: layer: 64 (over x, z, core), col: 4 (over y).
Axes of the slice: x: 4, y: 4, z: 8, core: 2. Of those that a mesh axis runs over, the one named last changes fastest.
Arguments:
- l_panels: bfloat16 [64, 2048, 2048], P('layer', None, 'col'), may hold values from -6 to 6
- u_panels: bfloat16 [64, 2048, 2048], P('layer', None, 'col'), may hold values from -0.125 to 0.125
- l_masks: int32 [64, 8, 8], P('layer'), may hold values 0 or 1
- u_masks: int32 [64, 8, 8], P('layer'), may hold values 0 or 1
- ancestor_tiles: int32 [8, 8], replicated, may hold values 0 or 1
- initial: float32 [2048, 2048], P('layer', 'col'), may hold values from -6 to 6
Outputs:
- schur: float32 [2048, 2048], P('layer', 'col')
All inputs are finite; a program needn't handle non-finite values. No bound on the sum of `l_masks` or of `u_masks` on one device may be relied on, other than what follows from the above.
Results may differ from a plain program's by a relative error of at most 0.0003.
Values may be sent and summed in bfloat16 or wider, within the bound.
A program may use at most 64 MiB of HBM per device.

v0:
```python
import jax
import jax.numpy as jnp
from jax import lax
from jax.sharding import PartitionSpec as P

TILE = 256


def expand_tiles(mask):
    return jnp.repeat(jnp.repeat(mask, TILE, 0), TILE, 1)


def local(l_panels, u_panels, l_masks, u_masks, ancestor_tiles, initial):
    col_index = lax.axis_index("col")
    depth_cols = l_panels.shape[2]
    width_cols = u_panels.shape[2]
    row_count = initial.shape[0]
    lmask_mine = lax.dynamic_slice_in_dim(
        l_masks[0], col_index * (depth_cols // TILE), depth_cols // TILE, 1
    )
    lpanel = l_panels[0] * expand_tiles(lmask_mine).astype(jnp.bfloat16)
    umask_mine = lax.dynamic_slice_in_dim(
        u_masks[0], col_index * (width_cols // TILE), width_cols // TILE, 1
    )
    upanel = u_panels[0] * expand_tiles(umask_mine).astype(jnp.bfloat16)
    full_panel = lax.all_gather(lpanel, "col", axis=1, tiled=True)
    product = jnp.dot(full_panel, upanel, preferred_element_type=jnp.float32)
    summed = lax.psum_scatter(product, "layer", scatter_dimension=0, tiled=True)
    row_ids = lax.axis_index("layer") * row_count + jnp.arange(row_count, dtype=jnp.int32)
    tile_ids = jnp.arange(ancestor_tiles.shape[0], dtype=jnp.int32)
    onehot = (row_ids[:, None] // TILE == tile_ids[None, :]).astype(jnp.float32)
    row_pattern = jnp.dot(
        onehot, ancestor_tiles.astype(jnp.float32), preferred_element_type=jnp.float32
    )
    col_pattern = lax.dynamic_slice_in_dim(
        row_pattern, col_index * (width_cols // TILE), width_cols // TILE, 1
    )
    pattern = jnp.repeat(col_pattern, TILE, 1)
    return initial - pattern * summed


def solution(mesh):
    return jax.shard_map(
        local,
        mesh=mesh,
        in_specs=(
            P("layer", None, "col"),
            P("layer", None, "col"),
            P("layer", None, None),
            P("layer", None, None),
            P(),
            P("layer", "col"),
        ),
        out_specs=P("layer", "col"),
        check_vma=False,
    )
```

profile of v0, /device:TPU:8, one launch (start us, length us, event | category | flops | bytes accessed | tf_op | source)
XLA Modules:
  0.0 265.6 jit_solution(10379563578866441089)
XLA Ops:
  6.5 0.0 all-gather.2.cloned.1.call-start
  6.5 0.8 fusion.4
  7.3 0.1 broadcast_in_dim.18
  7.4 2.5 broadcast_in_dim.19
  9.9 0.0 copy-start
  9.9 0.5 copy.15
  10.4 1.1 copy-done
  11.5 1.6 bitcast_multiply_fusion.2
  13.0 0.0 all-gather.2.cloned.1.call-update
  13.1 0.0 reduce-scatter.2.cloned.1.call-start
  13.1 0.1 broadcast_in_dim.20
  13.2 2.5 broadcast_in_dim.21
  15.7 0.5 copy.16
  16.2 85.6 %all-gather.2.cloned.1.call-done = bf16[2048,2048]{1,0:T(8,128)(2,1)} async-done(((bf16[2048,512]{1,0:T(8,128)(2,1)}), bf16[2048,2048]{1,0:T(8,128)(2,1)}) %all-gather.2.cloned.1.call-update) | async-done | bytes 8388624 | tf_op jit(solution)/shard_map/all_gather | solution.py:26
  101.8 10.5 %fusion = f32[2048,512]{1,0:T(8,128)} fusion(bf16[2048,2048]{1,0:T(8,128)(2,1)} %all-gather.2.cloned.1.call-done, bf16[2048,512]{1,0:T(8,128)(2,1)S(1)} %bitcast.23, bf16[1,2048,512]{2,1,0:T(8,128)(2,1)} %param.7), kind=kOutput, calls=%fused_computation.1 | convolution fusion | flops 4296015872 | bytes 16777216 | tf_op jit(solution)/shard_map/dot_general | solution.py:27
  112.2 0.0 copy-start.2
  112.2 0.0 copy-start.1
  112.2 0.0 reduce-scatter.2.cloned.1.call-update
  112.3 0.6 copy-done.2
  112.9 0.2 fusion.1
  113.1 0.1 copy.7
  113.2 0.1 broadcast_in_dim.17
  113.3 143.9 %reduce-scatter.2.cloned.1.call-done = f32[32,512]{1,0:T(8,128)} async-done(((f32[2048,512]{1,0:T(8,128)}), f32[32,512]{1,0:T(8,128)}) %reduce-scatter.2.cloned.1.call-update) | async-done | bytes 65552 | tf_op jit(solution)/shard_map/reduce_scatter | solution.py:28
  257.2 0.0 copy-done.1
  257.2 1.5 multiply_subtract_fusion
  (3 shorter events, 0.0 us)
Async XLA Ops:
  6.5 95.2 %all-gather.2.cloned.1.call-start = ((), (), s32[]{:S(2)}) async-start(), calls=%async_computation.1 | async-start | bytes 10485760 | tf_op jit(solution)/shard_map/all_gather | solution.py:26
  9.9 1.6 copy-start
  13.1 244.2 %reduce-scatter.2.cloned.1.call-start = ((), (), s32[]{:S(2)}) async-start(), calls=%async_computation.2 | async-start | bytes 4259840 | tf_op jit(solution)/shard_map/reduce_scatter | solution.py:28
  112.2 0.7 copy-start.2
  112.2 145.0 %copy-start.1 = (f32[32,512]{1,0:T(8,128)S(1)}, f32[32,512]{1,0:T(8,128)}, u32[]{:S(2)}) copy-start(f32[32,512]{1,0:T(8,128)} %param.11) | copy-start | bytes 196612
Sparse Core Ops, SparseCore 0:
  13.2 88.5 all-gather.1
  112.4 144.8 reduce-scatter.1
where the time goes:
time: 266 us
  waiting for transfers between devices  230 us (86%)
  between operations  13.5 us (5%)
  matrix products  10.6 us (4%)
  local copies, waits for them, and re-layouts  8.05 us (3%)
  other arithmetic  3.83 us (1%)
    reduce_scatter x1, waiting for transfers between devices, local(): summed = lax.psum_scatter(product, 'layer', scatter_dimension=0, tiled=True)  144 us
    all_gather x1, waiting for transfers between devices, local(): full_panel = lax.all_gather(lpanel, 'col', axis=1, tiled=True)  85.6 us
    dot_general x1, matrix products, local(): product = jnp.dot(full_panel, upanel, preferred_element_type=jnp.float32)  10.5 us
  transfers between devices with their start and end apart: 2, of which 2 were waited for; matrix products, arithmetic and copies ran while one was open for 1% of the time, Pallas kernels for 0%

commit v1 on v0

--- a/solution.py
+++ b/solution.py
@@ -23,7 +23,14 @@
         u_masks[0], col_index * (width_cols // TILE), width_cols // TILE, 1
     )
     upanel = u_panels[0] * expand_tiles(umask_mine).astype(jnp.bfloat16)
-    full_panel = lax.all_gather(lpanel, "col", axis=1, tiled=True)
+    devices = lax.axis_size("col")
+    right = [(i, (i + 1) % devices) for i in range(devices)]
+    parts = [lpanel]
+    for far in range(1, devices):
+        parts = [lax.ppermute(parts[0], "col", right), *parts]
+    whole = jnp.concatenate(parts, axis=1)
+    places = (lax.axis_index("col") + 1) * parts[-1].shape[1]
+    full_panel = jnp.roll(whole, places, axis=1)
     product = jnp.dot(full_panel, upanel, preferred_element_type=jnp.float32)
     summed = lax.psum_scatter(product, "layer", scatter_dimension=0, tiled=True)
     row_ids = lax.axis_index("layer") * row_count + jnp.arange(row_count, dtype=jnp.int32)

time: 266 us -> 325 us (1.22)
  waiting for transfers between devices: 230 us -> 278 us
  local copies, waits for them, and re-layouts: 8.05 us -> 19.7 us
  starting transfers between devices: 0.04 us -> 5 us
  matrix products: 10.6 us -> 6.18 us
    ppermute x0 -> x3, waiting for transfers between devices: none -> 130 us  [local(): parts = [lax.ppermute(parts[0], 'col', right), *parts]]
    all_gather x1 -> x0, waiting for transfers between devices: 85.6 us -> none  [local(): full_panel = lax.all_gather(lpanel, 'col', axis=1, tiled=True)]
    unnamed x9 -> x24, local copies, waits for them, and re-layouts: 2.76 us -> 14.2 us
    ppermute x0 -> x3, starting transfers between devices: none -> 5 us  [local(): parts = [lax.ppermute(parts[0], 'col', right), *parts]]
    dot_general x1, matrix products: 10.5 us -> 6 us  [local(): product = jnp.dot(full_panel, upanel, preferred_element_type=jnp.float32)]
    reduce_scatter x1, waiting for transfers between devices: 144 us -> 147 us  [local(): summed = lax.psum_scatter(product, 'layer', scatter_dimension=0, tiled=True)]
  transfers between devices with their start and end apart: 2 -> 4, of which waited for: 2 -> 4; matrix products, arithmetic and copies ran while one was open for 1% -> 1% of each run, Pallas kernels for 0% -> 0%
where the time goes in v1:
time: 325 us
  waiting for transfers between devices  278 us (86%)
  local copies, waits for them, and re-layouts  19.7 us (6%)
  between operations  13.6 us (4%)
  matrix products  6.18 us (2%)
  starting transfers between devices  5 us (2%)
    reduce_scatter x1, waiting for transfers between devices, local(): summed = lax.psum_scatter(product, 'layer', scatter_dimension=0, tiled=True)  147 us
    ppermute x3, waiting for transfers between devices, local(): parts = [lax.ppermute(parts[0], 'col', right), *parts]  130 us
    unnamed x24, local copies, waits for them, and re-layouts  14.2 us
  transfers between devices with their start and end apart: 4, of which 4 were waited for; matrix products, arithmetic and copies ran while one was open for 1% of the time, Pallas kernels for 0%

profile of v1, /device:TPU:8, one launch (start us, length us, event | category | flops | bytes accessed | tf_op | source)
XLA Modules:
  0.0 324.8 jit_solution(15249284741292936938)
XLA Ops:
  6.5 0.0 reduce-scatter.2.cloned.1.call-start
  6.5 0.0 copy-start.2
  6.5 0.9 fusion.5
  7.5 0.1 broadcast_in_dim.18
  7.5 2.5 broadcast_in_dim.19
  10.0 0.5 copy.15
  10.5 0.0 copy-done.2
  10.6 0.2 bitcast_multiply_fusion.2
  10.8 1.7 collective-permute-start
  12.4 45.8 %collective-permute-done = bf16[2048,512]{1,0:T(8,128)(2,1)S(1)} collective-permute-done((bf16[2048,512]{1,0:T(8,128)(2,1)S(1)}, bf16[2048,512]{1,0:T(8,128)(2,1)S(1)}, u32[]{:S(2)}, u32[]{:S(2)}) %collective-permute-start) | collective-permute-done | bytes 2097184 | tf_op jit(solution)/shard_map/ppermute | solution.py:30
  58.2 0.0 copy-start
  58.2 1.3 copy-done
  59.5 1.6 collective-permute-start.1
  61.1 44.8 %collective-permute-done.1 = bf16[2048,512]{1,0:T(8,128)(2,1)} collective-permute-done((bf16[2048,512]{1,0:T(8,128)(2,1)S(1)}, bf16[2048,512]{1,0:T(8,128)(2,1)}, u32[]{:S(2)}, u32[]{:S(2)}) %collective-permute-start.1) | collective-permute-done | bytes 2097184 | tf_op jit(solution)/shard_map/ppermute | solution.py:30
  106.0 1.8 collective-permute-start.2
  107.7 0.1 broadcast_in_dim.20
  107.8 2.5 broadcast_in_dim.21
  110.3 1.8 copy.16
  112.1 0.0 copy-start.1
  112.1 39.5 %collective-permute-done.2 = bf16[2048,512]{1,0:T(8,128)(2,1)} collective-permute-done((bf16[2048,512]{1,0:T(8,128)(2,1)}, bf16[2048,512]{1,0:T(8,128)(2,1)}, u32[]{:S(2)}, u32[]{:S(2)}) %collective-permute-start.2) | collective-permute-done | bytes 2097184 | tf_op jit(solution)/shard_map/ppermute | solution.py:30
  151.7 1.8 constant_dynamic-update-slice_fusion.7
  153.5 1.8 constant_dynamic-update-slice_fusion.6
  155.4 0.0 copy-done.1
  155.4 0.3 constant_dynamic-update-slice_fusion.5
  155.6 0.3 constant_dynamic-update-slice_fusion.4
  155.9 1.9 constant_dynamic-update-slice_fusion.3
  157.8 1.8 constant_dynamic-update-slice_fusion.2
  159.6 0.0 copy-start.3
  159.6 0.0 copy-start.5
  159.6 0.3 constant_dynamic-update-slice_fusion.1
  159.9 0.3 constant_dynamic-update-slice_fusion
  160.2 1.0 copy-done.3
  161.2 0.6 copy-done.5
  161.9 6.0 %fusion = f32[2048,512]{1,0:T(8,128)} fusion(bf16[2048,4096]{1,0:T(8,128)(2,1)S(1)} %constant_dynamic-update-slice_fusion, s32[]{:T(128)S(6)} %select_n.31, bf16[2048,512]{1,0:T(8,128)(2,1)S(1)} %bitcast.22, bf16[1,2048,512]{2,1,0:T(8,128)(2,1)S(1)} %copy-done.5), kind=kOutput, calls=%fused_computation | convolution fusion | flops 4296015872 | bytes 16777220 | tf_op jit(solution)/shard_map/dot_general | solution.py:34
  167.8 0.0 copy-start.6
  167.9 0.0 copy-start.4
  167.9 0.0 reduce-scatter.2.cloned.1.call-update
  167.9 0.6 copy-done.6
  168.5 0.2 fusion.2
  168.7 0.1 copy.7
  168.8 0.1 broadcast_in_dim.17
  169.0 147.5 %reduce-scatter.2.cloned.1.call-done = f32[32,512]{1,0:T(8,128)} async-done(((f32[2048,512]{1,0:T(8,128)}), f32[32,512]{1,0:T(8,128)}) %reduce-scatter.2.cloned.1.call-update) | async-done | bytes 65552 | tf_op jit(solution)/shard_map/reduce_scatter | solution.py:35
  316.4 0.0 copy-done.4
  316.4 1.5 multiply_subtract_fusion
  (3 shorter events, 0.0 us)
Async XLA Ops:
  6.5 309.9 %reduce-scatter.2.cloned.1.call-start = ((), (), s32[]{:S(2)}) async-start(), calls=%async_computation.1 | async-start | bytes 4259840 | tf_op jit(solution)/shard_map/reduce_scatter | solution.py:35
  6.5 4.0 %copy-start.2 = (bf16[1,2048,512]{2,1,0:T(8,128)(2,1)S(1)}, bf16[1,2048,512]{2,1,0:T(8,128)(2,1)}, u32[]{:S(2)}) copy-start(bf16[1,2048,512]{2,1,0:T(8,128)(2,1)} %param.6) | copy-start | bytes 6291460
  10.8 47.4 %collective-permute-start = (bf16[2048,512]{1,0:T(8,128)(2,1)S(1)}, bf16[2048,512]{1,0:T(8,128)(2,1)S(1)}, u32[]{:S(2)}, u32[]{:S(2)}) collective-permute-start(bf16[2048,512]{1,0:T(8,128)(2,1)S(1)} %bitcast_multiply_fusion.2), channel_id=1, source_target_pairs={{0,1},{1,2},{2,3},{3,0},{4,5},{5,6},{6,7},{7,4},{8,9},{9,10},{10,1... | collective-permute-start | bytes 6291464 | tf_op jit(solution)/shard_map/ppermute | solution.py:30
  58.2 1.3 copy-start
  59.5 46.4 %collective-permute-start.1 = (bf16[2048,512]{1,0:T(8,128)(2,1)S(1)}, bf16[2048,512]{1,0:T(8,128)(2,1)}, u32[]{:S(2)}, u32[]{:S(2)}) collective-permute-start(bf16[2048,512]{1,0:T(8,128)(2,1)S(1)} %collective-permute-done), channel_id=1, source_target_pairs={{0,1},{1,2},{2,3},{3,0},{4,5},{5,6},{6,7},{7,4},{8,9},{9,10},{10,1... | collective-permute-start | bytes 6291464 | tf_op jit(solution)/shard_map/ppermute | solution.py:30
  106.0 45.7 %collective-permute-start.2 = (bf16[2048,512]{1,0:T(8,128)(2,1)}, bf16[2048,512]{1,0:T(8,128)(2,1)}, u32[]{:S(2)}, u32[]{:S(2)}) collective-permute-start(bf16[2048,512]{1,0:T(8,128)(2,1)} %collective-permute-done.1), channel_id=1, source_target_pairs={{0,1},{1,2},{2,3},{3,0},{4,5},{5,6},{6,7},{7,4},{8,9},{9,10},{10,1... | collective-permute-start | bytes 6291464 | tf_op jit(solution)/shard_map/ppermute | solution.py:30
  112.1 43.2 %copy-start.1 = (bf16[2048,512]{1,0:T(8,128)(2,1)S(1)}, bf16[2048,512]{1,0:T(8,128)(2,1)}, u32[]{:S(2)}) copy-start(bf16[2048,512]{1,0:T(8,128)(2,1)} %copy-done) | copy-start | bytes 6291460
  159.6 1.6 copy-start.3
  159.6 2.2 copy-start.5
  167.8 0.7 copy-start.6
  167.9 148.6 %copy-start.4 = (f32[32,512]{1,0:T(8,128)S(1)}, f32[32,512]{1,0:T(8,128)}, u32[]{:S(2)}) copy-start(f32[32,512]{1,0:T(8,128)} %param.11) | copy-start | bytes 196612
Sparse Core Ops, SparseCore 0:
  168.0 148.3 reduce-scatter.1
